TPU v7x, 32 devices: a whole 2x2x4 slice. The times are simulated.
32 devices in a mesh: groups: 1, tensor: 16 (over z, y, x), sub: 2 (over core).
Axes of the slice: x: 2, y: 2, z: 4, core: 2. Of those that a mesh axis runs over, the one named last changes fastest.
Arguments:
- stored: bfloat16 [8192, 32768], P(('tensor', 'sub')), may hold values from -0.0625 to 0.0625
- tokens: bfloat16 [256, 8192], P(('groups', 'tensor')), may hold values from -6 to 6
- owner_map: int32 [256], replicated, may hold values from 0 to 255, each once
- live_count: int32 [1], P('groups'), may hold values from 128 to 256
Outputs:
- serving_out: bfloat16 [256, 32768], P('groups', ('tensor', 'sub'))
Inputs may be any that keep to these rules, and one draw needn't show every extreme that they name: `owner_map`: each of the 256 saved column blocks is named exactly once. Rows from live_count on are padding.
All inputs are finite; a program needn't handle non-finite values.
Results may differ from a plain program's by a relative error of at most 0.001.
Values may be sent and summed in bfloat16 or wider, within the bound.
No kernel may reach another device: no remote copies, remote signals or barrier semaphores. Data moves between devices by JAX's collectives and lax.ppermute only.
A program may use at most 128 MiB of HBM per device.

v0:
```python
import jax
import jax.numpy as jnp
from jax import lax
from jax.sharding import PartitionSpec as P


def on_device(stored, tokens, owner_map, live_count):
    row_count = stored.shape[0]
    block_count = owner_map.shape[0]
    width = stored.shape[1] // block_count
    devices = lax.axis_size(("tensor", "sub"))
    per_dev = block_count // devices
    ordered = jnp.take(stored.reshape(row_count, block_count, width), owner_map, axis=1)
    gathered = lax.all_gather(tokens, "tensor", axis=0, tiled=True)
    sectioned = ordered.reshape(row_count, devices, per_dev, width)
    piece = lax.all_to_all(sectioned, ("tensor", "sub"), split_axis=1, concat_axis=0, tiled=True)
    weights = piece.reshape(piece.shape[0], piece.shape[2], piece.shape[3])
    result = jnp.einsum("td,dkc->tkc", gathered, weights, preferred_element_type=jnp.float32)
    product = result.reshape(result.shape[0], per_dev * width)
    row_ids = lax.broadcasted_iota(jnp.int32, (product.shape[0], 1), 0)
    keep = row_ids < live_count[0]
    return jnp.where(keep, product, jnp.float32(0.0)).astype(jnp.bfloat16)


def solution(mesh):
    placed = (P(("tensor", "sub"), None), P(("groups", "tensor"), None), P(), P("groups"))
    return jax.shard_map(
        on_device,
        mesh=mesh,
        in_specs=placed,
        out_specs=P("groups", ("tensor", "sub")),
        check_vma=False,
    )
```

profile of v0, /device:TPU:0, one launch (start us, length us, event | category | flops | bytes accessed | tf_op | source)
XLA Modules:
  0.0 527.3 jit_solution(14248439712817356019)
XLA Ops:
  6.5 0.7 compare_select_fusion
  7.2 0.7 compare_and_fusion
  7.9 22.3 %copy.14 = bf16[256,32768]{0,1:T(8,128)(2,1)} copy(bf16[256,32768]{1,0:T(8,128)(2,1)} %param.4) | data formatting | bytes 33554432 | tf_op args[0]
  30.3 22.4 %copy.15 = bf16[256,256,128]{2,0,1:T(8,128)(2,1)} copy(bf16[256,256,128]{0,2,1:T(8,128)(2,1)} %bitcast.18) | data formatting | bytes 33554432 | tf_op jit(solution)/shard_map/reshape | solution.py:13
  52.6 0.1 broadcast_in_dim.27
  52.7 15.5 %gather_fusion = bf16[256,256,128]{2,1,0:T(8,128)(2,1)} fusion(bf16[256,256,128]{2,0,1:T(8,128)(2,1)} %copy.15, s32[1024]{0:T(1024)S(1)} %pad_clamp_fusion), kind=kCustom, calls=%fused_computation | custom fusion | bytes 33555456 | tf_op jit(solution)/shard_map/jit(_take)/gather | solution.py:13
  68.3 14.9 %bitcast_select_fusion = bf16[256,32,8,128]{3,2,1,0:T(8,128)(2,1)S(1)} fusion(bf16[256,256,128]{2,0,1:T(8,128)(2,1)} %bitcast.17, pred[32,8]{1,0:T(8,128)(4,1)S(1)} %broadcast_in_dim.27), kind=kLoop, calls=%fused_computation.3 | loop fusion | flops 8388608 | bytes 33554688 | tf_op jit(solution)/shard_map/jit(_take)/select_n | solution.py:13
  83.1 7.4 %copy.17 = bf16[256,32,8,128]{3,2,0,1:T(8,128)(2,1)} copy(bf16[256,32,8,128]{3,2,1,0:T(8,128)(2,1)S(1)} %bitcast_select_fusion) | data formatting | bytes 33554432 | tf_op jit(solution)/shard_map/jit(_take)/select_n | solution.py:13
  90.5 7.4 %all-to-all-start = ((bf16[256,32,8,128]{3,2,0,1:T(8,128)(2,1)}), bf16[256,32,8,128]{3,2,0,1:T(8,128)(2,1)}, u32[]{:S(2)}, u32[]{:S(2)}) async-start(bf16[256,32,8,128]{3,2,0,1:T(8,128)(2,1)} %copy.17), calls=%async_computation | async-start | bytes 33554432 | tf_op jit(solution)/shard_map/all_to_all | solution.py:16
  98.0 0.0 all-gather.2.cloned.1.call-start
  98.0 0.7 all-gather.2.cloned.1.call-update
  99.3 208.4 %all-gather.2.cloned.1.call-done = bf16[256,8192]{1,0:T(8,128)(2,1)} async-done(((bf16[16,8192]{1,0:T(8,128)(2,1)}), bf16[256,8192]{1,0:T(8,128)(2,1)}) %all-gather.2.cloned.1.call-update) | async-done | bytes 4194320 | tf_op jit(solution)/shard_map/all_gather | solution.py:14
  307.7 199.8 %all-to-all-done = bf16[256,32,8,128]{3,2,0,1:T(8,128)(2,1)} async-done(((bf16[256,32,8,128]{3,2,0,1:T(8,128)(2,1)}), bf16[256,32,8,128]{3,2,0,1:T(8,128)(2,1)}, u32[]{:S(2)}, u32[]{:S(2)}) %all-to-all-start) | async-done | bytes 16777248 | tf_op jit(solution)/shard_map/all_to_all | solution.py:16
  507.6 11.7 %fusion = bf16[8,128,256]{2,1,0:T(8,128)(2,1)S(1)} fusion(bf16[8192,8,128]{2,1,0:T(8,128)(2,1)} %bitcast.6, bf16[256,8192]{1,0:T(8,128)(2,1)} %all-gather.2.cloned.1.call-done), kind=kOutput, calls=%fused_computation.1 | convolution fusion | flops 4294967296 | bytes 21495808 | tf_op jit(solution)/shard_map/td,dkc->tkc/dot_general | solution.py:18
  519.3 0.2 copy.19
  519.5 1.0 select_convert_fusion
  (2 shorter events, 0.0 us)
Async XLA Ops:
  90.5 417.0 %all-to-all-start = ((bf16[256,32,8,128]{3,2,0,1:T(8,128)(2,1)}), bf16[256,32,8,128]{3,2,0,1:T(8,128)(2,1)}, u32[]{:S(2)}, u32[]{:S(2)}) async-start(bf16[256,32,8,128]{3,2,0,1:T(8,128)(2,1)} %copy.17), calls=%async_computation | async-start | bytes 33554432 | tf_op jit(solution)/shard_map/all_to_all | solution.py:16
  98.0 209.8 %all-gather.2.cloned.1.call-start = ((), (), s32[]{:S(2)}) async-start(), calls=%async_computation.1 | async-start | bytes 4456448 | tf_op jit(solution)/shard_map/all_gather | solution.py:14
Sparse Core Ops, SparseCore 0:
  101.6 206.1 all-gather.1
where the time goes:
time: 529 us; the launch traced here: 527 us
  waiting for transfers between devices  409 us (77%)
  local copies, waits for them, and re-layouts  67.9 us (13%)
  other arithmetic  17.2 us (3%)
  between operations  14.1 us (3%)
  matrix products  11.7 us (2%)
  starting transfers between devices  7.47 us (1%)
    all_gather x1, waiting for transfers between devices, on_device(): gathered = lax.all_gather(tokens, 'tensor', axis=0, tiled=True)  208 us
    all_to_all x1, waiting for transfers between devices, on_device(): lax.all_to_all(sectioned, ('tensor', 'sub'), split_axis=1, concat_axis=0,...  200 us
    reshape x1, local copies, waits for them, and re-layouts, on_device(): stored.reshape(row_count, block_count, width)  22.4 us
    unnamed x1, local copies, waits for them, and re-layouts  22.3 us
    select_n x2, other arithmetic, on_device(): jnp.take(stored.reshape(row_count, block_count, width), owner_map, axis=1)  15.5 us
    gather x1, local copies, waits for them, and re-layouts, on_device(): jnp.take(stored.reshape(row_count, block_count, width), owner_map, axis=1)  15.5 us
    dot_general x1, matrix products, on_device(): jnp.einsum('td,dkc->tkc', gathered, weights, preferred_element_type=jnp.f...  11.7 us
  transfers between devices with their start and end apart: 2, of which 2 were waited for; matrix products, arithmetic and copies ran while one was open for 0% of the time, Pallas kernels for 0%

commit v1 on v0

v1 whole, which is shorter than its diff:
```python
import functools

import jax
import jax.numpy as jnp
from jax import lax
from jax.experimental import pallas as pl
from jax.experimental.pallas import tpu as pltpu
from jax.sharding import PartitionSpec as P

STEPS = 128.0
TOP = 32000.0
TILE = 16
VMEM = 40 * 1024 * 1024


def flow_orders(bits):
    straight = list(range(bits))
    orders = [straight, straight[1:] + straight[:1], straight[2:3] + straight[:2] + straight[3:]]
    return orders[: max(1, min(3, bits))]


def flow_blocks(per_dev, flows):
    flows = min(flows, per_dev)
    counts = [per_dev // flows + (1 if f < per_dev % flows else 0) for f in range(flows)]
    firsts = [sum(counts[:f]) for f in range(flows)]
    return list(zip(firsts, counts))


class Flow:
    def __init__(self, order, first, count, per_dev, width, chips):
        self.order, self.first, self.count = order, first, count
        self.per_dev, self.width, self.chips = per_dev, width, chips
        self.bits = len(order)
        self.cols = count * width

    def block_id(self, owner, meta, place, j, sub):
        flipped = 0
        for s, bit in enumerate(self.order):
            flipped = flipped + (((place >> (self.bits - 1 - s)) & 1) << bit)
        dest = meta[0] ^ flipped
        return owner[(dest * 2 + sub) * self.per_dev + self.first + j]

    def send_range(self, stage):
        return self.chips >> (stage + 1)


def gather_kernel(n, owner, meta, *refs):
    out = refs[n]
    width = refs[0].shape[1]
    for k in range(n):
        out[:, k * width:(k + 1) * width] = refs[k][...]


def gather_for_sibling(stored, owner, meta, flow, low, count):
    rows = stored.shape[0]
    group = min(count, 4)
    n = group * flow.count

    def pick(k, i, owner, meta):
        return 0, flow.block_id(owner, meta, low + i * group + k // flow.count, k % flow.count, 1 - meta[1])

    return pl.pallas_call(
        functools.partial(gather_kernel, n),
        grid_spec=pltpu.PrefetchScalarGridSpec(
            num_scalar_prefetch=2,
            grid=(count // group,),
            in_specs=[pl.BlockSpec((rows, flow.width), functools.partial(pick, k)) for k in range(n)],
            out_specs=pl.BlockSpec((rows, n * flow.width), lambda i, owner, meta: (0, i)),
        ),
        out_shape=jax.ShapeDtypeStruct((rows, count * flow.cols), stored.dtype),
        compiler_params=pltpu.CompilerParams(vmem_limit_bytes=VMEM),
        cost_estimate=pl.CostEstimate(flops=0, bytes_accessed=4 * rows * count * flow.cols, transcendentals=0),
    )(owner, meta, *[stored] * n)


def decode_scale(code):
    return jnp.exp2(code * (1.0 / STEPS)) * (1.0 / TOP)


def partial_sum(n, prev, tok_own, tok_sib, refs):
    own = jnp.concatenate([refs[k][...] for k in range(n)], axis=1)
    total = jnp.dot(tok_own[...], own, preferred_element_type=jnp.float32)
    total = total + jnp.dot(tok_sib[...], refs[n][...], preferred_element_type=jnp.float32)
    main = total.shape[0] - TILE
    body, tail = total[:main], total[main:]
    for ref in refs[n + 1:n + 1 + prev]:
        last = ref[main:, :].astype(jnp.float32)
        scale = decode_scale(last[TILE - 1:, :])
        body = body + ref[:main, :].astype(jnp.float32) * scale
        tail = tail + last * scale
    return body, tail


def send_kernel(n, prev, owner, meta, tok_own, tok_sib, *refs):
    out = refs[n + 1 + prev]
    body, tail = partial_sum(n, prev, tok_own, tok_sib, refs)
    main = body.shape[0]
    is_code = lax.broadcasted_iota(jnp.int32, tail.shape, 0) == TILE - 1
    tail = jnp.where(is_code, 0.0, tail)
    top = jnp.maximum(jnp.max(jnp.abs(body), axis=0, keepdims=True), jnp.max(jnp.abs(tail), axis=0, keepdims=True))
    code = jnp.ceil(jnp.log2(jnp.maximum(top, 1e-30)) * STEPS)
    up = 1.0 / decode_scale(code)
    out[:main, :] = jnp.round(body * up).astype(jnp.int32).astype(jnp.int16)
    out[main:, :] = jnp.where(is_code, code, jnp.round(tail * up)).astype(jnp.int32).astype(jnp.int16)


def send_part(stored, owner, meta, tokens, sibling, arrived, flow, stage, low):
    rows = stored.shape[0]
    places = flow.send_range(stage)
    group = min(places, 2)
    n = group * flow.count
    cols = group * flow.cols
    height = tokens.shape[0]

    def pick(k, i, owner, meta):
        return 0, flow.block_id(owner, meta, places + i * group + k // flow.count, k % flow.count, meta[1])

    at = lambda first: (lambda i, owner, meta: (0, first // group + i))
    return pl.pallas_call(
        functools.partial(send_kernel, n, len(arrived)),
        grid_spec=pltpu.PrefetchScalarGridSpec(
            num_scalar_prefetch=2,
            grid=(places // group,),
            in_specs=[
                pl.BlockSpec((height, rows), lambda i, owner, meta: (0, meta[1])),
                pl.BlockSpec((height, rows), lambda i, owner, meta: (0, 1 - meta[1])),
                *[pl.BlockSpec((rows, flow.width), functools.partial(pick, k)) for k in range(n)],
                pl.BlockSpec((rows, cols), at(places - low)),
                *[pl.BlockSpec((height, cols), at(places)) for _ in arrived],
            ],
            out_specs=pl.BlockSpec((height, cols), at(0)),
        ),
        out_shape=jax.ShapeDtypeStruct((height, places * flow.cols), jnp.int16),
        compiler_params=pltpu.CompilerParams(vmem_limit_bytes=VMEM),
        cost_estimate=pl.CostEstimate(
            flops=4 * height * rows * places * flow.cols,
            bytes_accessed=(4 * rows + 2 * height * (1 + len(arrived))) * places * flow.cols,
            transcendentals=0,
        ),
    )(owner, meta, tokens, tokens, *[stored] * n, sibling, *arrived)


def last_kernel(flows, owner, meta, tok_own, tok_sib, *refs):
    out = refs[-1]
    live = meta[2]
    at = 0
    for flow in flows:
        body, tail = partial_sum(flow.count, flow.bits, tok_own, tok_sib, refs[at:])
        at += flow.count + 1 + flow.bits
        cols = slice(flow.first * flow.width, flow.first * flow.width + flow.cols)
        for first, part in ((0, body), (body.shape[0], tail)):
            size = min(part.shape[0], out.shape[0] - first)
            if size > 0:
                ids = first + lax.broadcasted_iota(jnp.int32, (size, part.shape[1]), 0)
                out[first:first + size, cols] = jnp.where(ids < live, part[:size], 0.0).astype(out.dtype)
        done = body.shape[0] + tail.shape[0]
        if done < out.shape[0]:
            out[done:, cols] = jnp.zeros((out.shape[0] - done, flow.cols), out.dtype)


def last_part(stored, owner, meta, tokens, siblings, arrived, flows, count):
    rows, height = stored.shape[0], tokens.shape[0]
    specs = [
        pl.BlockSpec((height, rows), lambda i, owner, meta: (0, meta[1])),
        pl.BlockSpec((height, rows), lambda i, owner, meta: (0, 1 - meta[1])),
    ]
    operands = [tokens, tokens]
    for flow, sibling, got in zip(flows, siblings, arrived):
        for j in range(flow.count):
            specs.append(pl.BlockSpec(
                (rows, flow.width),
                functools.partial(lambda f, j, i, owner, meta: (0, f.block_id(owner, meta, 0, j, meta[1])), flow, j)))
            operands.append(stored)
        specs.append(pl.BlockSpec((rows, flow.cols), lambda i, owner, meta: (0, 0)))
        operands.append(sibling)
        for part in got:
            specs.append(pl.BlockSpec((height, flow.cols), lambda i, owner, meta: (0, 0)))
            operands.append(part)
    cols = sum(flow.cols for flow in flows)
    return pl.pallas_call(
        functools.partial(last_kernel, flows),
        grid_spec=pltpu.PrefetchScalarGridSpec(
            num_scalar_prefetch=2,
            grid=(1,),
            in_specs=specs,
            out_specs=pl.BlockSpec((count, cols), lambda i, owner, meta: (0, 0)),
        ),
        out_shape=jax.ShapeDtypeStruct((count, cols), jnp.bfloat16),
        compiler_params=pltpu.CompilerParams(vmem_limit_bytes=VMEM),
    )(owner, meta, *operands)


def on_device(stored, tokens, owner_map, live_count):
    rows = stored.shape[0]
    block_count = owner_map.shape[0]
    width = stored.shape[1] // block_count
    chips = lax.axis_size("tensor")
    per_dev = block_count // (2 * chips)
    count = tokens.shape[0] * chips
    bits = chips.bit_length() - 1
    orders = flow_orders(bits)
    flows = [
        Flow(order, first, blocks, per_dev, width, chips)
        for order, (first, blocks) in zip(orders, flow_blocks(per_dev, len(orders)))
    ]
    meta = jnp.stack([lax.axis_index("tensor"), lax.axis_index("sub"), live_count[0]]).astype(jnp.int32)

    half = chips // 2
    swap = [(0, 1), (1, 0)]
    far = [lax.ppermute(gather_for_sibling(stored, owner_map, meta, f, half, half), "sub", swap) for f in flows]
    near = [lax.ppermute(gather_for_sibling(stored, owner_map, meta, f, 0, half), "sub", swap) for f in flows]

    part = lax.all_to_all(tokens, "tensor", split_axis=1, concat_axis=0, tiled=True)
    ids = lax.broadcasted_iota(jnp.int32, (count, 1), 0)
    part = jnp.where(ids < live_count[0], part, jnp.zeros((), part.dtype))
    height = count + TILE
    part = jnp.pad(part, ((0, height - count), (0, 0)))

    arrived = [[] for _ in flows]
    for stage in range(bits):
        for f, flow in enumerate(flows):
            low = half if stage == 0 else 0
            sent = send_part(stored, owner_map, meta, part, (far if stage == 0 else near)[f], arrived[f], flow, stage, low)
            step = 1 << flow.order[stage]
            arrived[f].append(lax.ppermute(sent, "tensor", [(c, c ^ step) for c in range(chips)]))
    return last_part(stored, owner_map, meta, part, near, arrived, flows, count)


def solution(mesh):
    placed = (P(("tensor", "sub"), None), P(("groups", "tensor"), None), P(), P("groups"))
    return jax.shard_map(
        on_device,
        mesh=mesh,
        in_specs=placed,
        out_specs=P("groups", ("tensor", "sub")),
        check_vma=False,
    )
```

time: 529 us -> 139 us (0.26)
  waiting for transfers between devices: 409 us -> 53.2 us
  local copies, waits for them, and re-layouts: 67.9 us -> 1.44 us
  Pallas kernels: 0 us -> 55.4 us
  starting transfers between devices: 7.47 us -> 26.2 us
  other arithmetic: 17.2 us -> 0.18 us
  between operations: 14.1 us -> 0.87 us
  matrix products: 11.7 us -> 0 us
    all_gather x1 -> x0, waiting for transfers between devices: 208 us -> none  [on_device(): gathered = lax.all_gather(tokens, 'tensor', axis=0, tiled=True)]
    all_to_all x1, waiting for transfers between devices: 200 us -> 3.12 us  [on_device(): lax.all_to_all(tokens, 'tensor', split_axis=1, concat_axis=0, tiled=True)]
    pallas_call x0 -> x19, Pallas kernels: none -> 55.4 us  [the longest x12 34.6 us: send_part(): pl.pallas_call(functools.partial(send_kernel, n, len(arrived)), grid_spec...]
    ppermute x0 -> x18, waiting for transfers between devices: none -> 50.1 us  [the longest x12 50.1 us: on_device(): lax.ppermute(sent, 'tensor', [(c, c ^ step) for c in range(chips)])]
    reshape x2 -> x0, local copies, waits for them, and re-layouts: 22.6 us -> none  [the longest x1 22.4 us: on_device(): stored.reshape(row_count, block_count, width)]
    unnamed x1 -> x6, local copies, waits for them, and re-layouts: 22.3 us -> 0.69 us
    ppermute x0 -> x18, starting transfers between devices: none -> 17.9 us  [the longest x12 16.3 us: on_device(): lax.ppermute(sent, 'tensor', [(c, c ^ step) for c in range(chips)])]
    gather x1 -> x0, local copies, waits for them, and re-layouts: 15.5 us -> none  [on_device(): jnp.take(stored.reshape(row_count, block_count, width), owner_map, axis=1)]
  transfers between devices with their start and end apart: 2 -> 19, of which waited for: 2 -> 6; matrix products, arithmetic and copies ran while one was open for 0% -> 1% of each run, Pallas kernels for 0% -> 35%
where the time goes in v1:
time: 139 us; the launch traced here: 137 us
  Pallas kernels  55.4 us (40%)
  waiting for transfers between devices  53.2 us (38%)
  starting transfers between devices  26.2 us (19%)
  local copies, waits for them, and re-layouts  1.44 us (1%)
    ppermute x12, waiting for transfers between devices, on_device(): lax.ppermute(sent, 'tensor', [(c, c ^ step) for c in range(chips)])  50.1 us
    pallas_call x12, Pallas kernels, send_part(): pl.pallas_call(functools.partial(send_kernel, n, len(arrived)), grid_spec...  34.6 us
    pallas_call x6, Pallas kernels, gather_for_sibling(): pl.pallas_call(functools.partial(gather_kernel, n), grid_spec=pltpu.Prefe...  17.5 us
    ppermute x12, starting transfers between devices, on_device(): lax.ppermute(sent, 'tensor', [(c, c ^ step) for c in range(chips)])  16.3 us
    all_to_all x1, starting transfers between devices, on_device(): lax.all_to_all(tokens, 'tensor', split_axis=1, concat_axis=0, tiled=True)  8.31 us
    pallas_call x1, Pallas kernels, last_part(): pl.pallas_call(functools.partial(last_kernel, flows), grid_spec=pltpu.Pre...  3.36 us
    all_to_all x1, waiting for transfers between devices, on_device(): lax.all_to_all(tokens, 'tensor', split_axis=1, concat_axis=0, tiled=True)  3.12 us
  transfers between devices with their start and end apart: 19, of which 6 were waited for; matrix products, arithmetic and copies ran while one was open for 1% of the time, Pallas kernels for 35%

profile of v1, /device:TPU:0, one launch (start us, length us, event | category | flops | bytes accessed | tf_op | source)
XLA Modules:
  0.0 137.3 jit_solution(140591090696173229)
XLA Ops:
  1.4 3.4 %shard_map.53 = bf16[256,3072]{1,0:T(8,128)(2,1)} custom-call(s32[256]{0:T(256)S(1)} %copy-done, s32[3]{0:T(128)S(1)} %pad_add_fusion.meta, bf16[256,32768]{1,0:T(8,128)(2,1)} %refs_17_.1, bf16[256,32768]{1,0:T(8,128)(2,1)} %refs_17_.1, bf16[256,32768]{1,0:T(8,128)(2,1)} %refs_17_.1, bf16[256,32768]{1,0:T(8,128)(2,1)} %refs_17_.1, ...), custom_call_target="tpu_custom_call" | custom-call | bytes 3145728 | tf_op jit(solution)/shard_map/pallas_call | solution.py:62
  5.4 2.7 %shard_map.47 = bf16[256,3072]{1,0:T(8,128)(2,1)S(1)} custom-call(s32[256]{0:T(256)S(1)} %copy-done, s32[3]{0:T(128)S(1)} %pad_add_fusion.meta, bf16[256,32768]{1,0:T(8,128)(2,1)} %refs_17_.1, bf16[256,32768]{1,0:T(8,128)(2,1)} %refs_17_.1, bf16[256,32768]{1,0:T(8,128)(2,1)} %refs_17_.1, bf16[256,32768]{1,0:T(8,128)(2,1)} %refs_17_.1, ...), custom_call_target="tpu_custom_call" | custom-call | bytes 3145728 | tf_op jit(solution)/shard_map/pallas_call | solution.py:62
  8.9 8.3 %all-to-all-start = ((bf16[16,16,512]{2,0,1:T(8,128)(2,1)}), bf16[16,16,512]{2,0,1:T(8,128)(2,1)S(1)}, u32[]{:S(2)}, u32[]{:S(2)}) async-start(bf16[16,16,512]{2,0,1:T(8,128)(2,1)} %bitcast.12), calls=%async_computation | async-start | bytes 524288 | tf_op jit(solution)/shard_map/all_to_all | solution.py:213
  17.2 3.0 %shard_map.59 = bf16[256,2048]{1,0:T(8,128)(2,1)} custom-call(s32[256]{0:T(256)S(1)} %copy-done.1, s32[3]{0:T(128)S(1)} %pad_add_fusion.meta, bf16[256,32768]{1,0:T(8,128)(2,1)} %refs_17_.1, bf16[256,32768]{1,0:T(8,128)(2,1)} %refs_17_.1, bf16[256,32768]{1,0:T(8,128)(2,1)} %refs_17_.1, bf16[256,32768]{1,0:T(8,128)(2,1)} %refs_17_.1, ...), custom_call_target="tpu_custom_call" | custom-call | bytes 2097152 | tf_op jit(solution)/shard_map/pallas_call | solution.py:62
  20.3 3.3 %shard_map.52 = bf16[256,3072]{1,0:T(8,128)(2,1)} custom-call(s32[256]{0:T(256)S(1)} %copy-done.1, s32[3]{0:T(128)S(1)} %pad_add_fusion.meta, bf16[256,32768]{1,0:T(8,128)(2,1)} %refs_17_.1, bf16[256,32768]{1,0:T(8,128)(2,1)} %refs_17_.1, bf16[256,32768]{1,0:T(8,128)(2,1)} %refs_17_.1, bf16[256,32768]{1,0:T(8,128)(2,1)} %refs_17_.1, ...), custom_call_target="tpu_custom_call" | custom-call | bytes 3145728 | tf_op jit(solution)/shard_map/pallas_call | solution.py:62
  24.2 3.1 %all-to-all-done = bf16[16,16,512]{2,0,1:T(8,128)(2,1)S(1)} async-done(((bf16[16,16,512]{2,0,1:T(8,128)(2,1)}), bf16[16,16,512]{2,0,1:T(8,128)(2,1)S(1)}, u32[]{:S(2)}, u32[]{:S(2)}) %all-to-all-start) | async-done | bytes 262176 | tf_op jit(solution)/shard_map/all_to_all | solution.py:213
  27.4 4.9 %shard_map.54 = s16[272,3072]{1,0:T(8,128)(2,1)S(1)} custom-call(s32[256]{0:T(256)S(1)} %copy-done.1, s32[3]{0:T(128)S(1)} %pad_add_fusion.meta, bf16[272,512]{1,0:T(8,128)(2,1)S(1)} %pad.4.tok_own.tok_sib, bf16[272,512]{1,0:T(8,128)(2,1)S(1)} %pad.4.tok_own.tok_sib, bf16[256,32768]{1,0:T(8,128)(2,1)} %refs_17_.1, bf16[256,32768]{1,0:T(8,128)(2,1)} %refs_17_.1, ...), custom_call_target="tpu_custom_call" | custom-call | flops 855638016 | bytes 4816896 | tf_op jit(solution)/shard_map/pallas_call | solution.py:119
  33.4 4.6 %shard_map.48 = s16[272,3072]{1,0:T(8,128)(2,1)S(1)} custom-call(s32[256]{0:T(256)S(1)} %copy-done.1, s32[3]{0:T(128)S(1)} %pad_add_fusion.meta, bf16[272,512]{1,0:T(8,128)(2,1)S(1)} %pad.4.tok_own.tok_sib, bf16[272,512]{1,0:T(8,128)(2,1)S(1)} %pad.4.tok_own.tok_sib, bf16[256,32768]{1,0:T(8,128)(2,1)} %refs_17_.1, bf16[256,32768]{1,0:T(8,128)(2,1)} %refs_17_.1, ...), custom_call_target="tpu_custom_call" | custom-call | flops 855638016 | bytes 4816896 | tf_op jit(solution)/shard_map/pallas_call | solution.py:119
  38.6 2.7 %shard_map.46 = bf16[256,3072]{1,0:T(8,128)(2,1)S(1)} custom-call(s32[256]{0:T(256)S(1)} %copy-done.1, s32[3]{0:T(128)S(1)} %pad_add_fusion.meta, bf16[256,32768]{1,0:T(8,128)(2,1)} %refs_17_.1, bf16[256,32768]{1,0:T(8,128)(2,1)} %refs_17_.1, bf16[256,32768]{1,0:T(8,128)(2,1)} %refs_17_.1, bf16[256,32768]{1,0:T(8,128)(2,1)} %refs_17_.1, ...), custom_call_target="tpu_custom_call" | custom-call | bytes 3145728 | tf_op jit(solution)/shard_map/pallas_call | solution.py:62
  41.4 4.3 %shard_map.60 = s16[272,2048]{1,0:T(8,128)(2,1)S(1)} custom-call(s32[256]{0:T(256)S(1)} %copy-done.1, s32[3]{0:T(128)S(1)} %pad_add_fusion.meta, bf16[272,512]{1,0:T(8,128)(2,1)S(1)} %pad.4.tok_own.tok_sib, bf16[272,512]{1,0:T(8,128)(2,1)S(1)} %pad.4.tok_own.tok_sib, bf16[256,32768]{1,0:T(8,128)(2,1)} %refs_17_.1, bf16[256,32768]{1,0:T(8,128)(2,1)} %refs_17_.1, ...), custom_call_target="tpu_custom_call" | custom-call | flops 570425344 | bytes 3211264 | tf_op jit(solution)/shard_map/pallas_call | solution.py:119
  46.7 2.4 %shard_map.58 = bf16[256,2048]{1,0:T(8,128)(2,1)S(1)} custom-call(s32[256]{0:T(256)S(1)} %copy-done.1, s32[3]{0:T(128)S(1)} %pad_add_fusion.meta, bf16[256,32768]{1,0:T(8,128)(2,1)} %refs_17_.1, bf16[256,32768]{1,0:T(8,128)(2,1)} %refs_17_.1, bf16[256,32768]{1,0:T(8,128)(2,1)} %refs_17_.1, bf16[256,32768]{1,0:T(8,128)(2,1)} %refs_17_.1, ...), custom_call_target="tpu_custom_call" | custom-call | bytes 2097152 | tf_op jit(solution)/shard_map/pallas_call | solution.py:62
  49.4 19.3 %collective-permute-done.8.refs_7_.refs_4_.refs_12_ = s16[272,3072]{1,0:T(8,128)(2,1)S(1)} collective-permute-done((s16[272,3072]{1,0:T(8,128)(2,1)S(1)}, s16[272,3072]{1,0:T(8,128)(2,1)S(1)}, u32[]{:S(2)}, u32[]{:S(2)}) %collective-permute-start.8) | collective-permute-done | bytes 1671200 | tf_op jit(solution)/shard_map/ppermute | solution.py:225
  68.7 3.1 %shard_map.55 = s16[272,1536]{1,0:T(8,128)(2,1)S(1)} custom-call(s32[256]{0:T(256)S(1)} %copy-done.1, s32[3]{0:T(128)S(1)} %pad_add_fusion.meta, bf16[272,512]{1,0:T(8,128)(2,1)S(1)} %pad.4.tok_own.tok_sib, bf16[272,512]{1,0:T(8,128)(2,1)S(1)} %pad.4.tok_own.tok_sib, bf16[256,32768]{1,0:T(8,128)(2,1)} %refs_17_.1, bf16[256,32768]{1,0:T(8,128)(2,1)} %refs_17_.1, ...), custom_call_target="tpu_custom_call" | custom-call | flops 427819008 | bytes 3244032 | tf_op jit(solution)/shard_map/pallas_call | solution.py:119
  72.9 1.2 collective-permute-done.2.refs_7_.refs_4_
  74.1 2.9 %shard_map.49 = s16[272,1536]{1,0:T(8,128)(2,1)S(1)} custom-call(s32[256]{0:T(256)S(1)} %copy-done.1, s32[3]{0:T(128)S(1)} %pad_add_fusion.meta, bf16[272,512]{1,0:T(8,128)(2,1)S(1)} %pad.4.tok_own.tok_sib, bf16[272,512]{1,0:T(8,128)(2,1)S(1)} %pad.4.tok_own.tok_sib, bf16[256,32768]{1,0:T(8,128)(2,1)} %refs_17_.1, bf16[256,32768]{1,0:T(8,128)(2,1)} %refs_17_.1, ...), custom_call_target="tpu_custom_call" | custom-call | flops 427819008 | bytes 3244032 | tf_op jit(solution)/shard_map/pallas_call | solution.py:119
  77.0 1.1 collective-permute-start.3
  78.2 2.6 %shard_map.61 = s16[272,1024]{1,0:T(8,128)(2,1)S(1)} custom-call(s32[256]{0:T(256)S(1)} %copy-done.1, s32[3]{0:T(128)S(1)} %pad_add_fusion.meta, bf16[272,512]{1,0:T(8,128)(2,1)S(1)} %pad.4.tok_own.tok_sib, bf16[272,512]{1,0:T(8,128)(2,1)S(1)} %pad.4.tok_own.tok_sib, bf16[256,32768]{1,0:T(8,128)(2,1)} %refs_17_.1, bf16[256,32768]{1,0:T(8,128)(2,1)} %refs_17_.1, ...), custom_call_target="tpu_custom_call" | custom-call | flops 285212672 | bytes 2162688 | tf_op jit(solution)/shard_map/pallas_call | solution.py:119
  80.8 1.8 %collective-permute-start.15 = (s16[272,1024]{1,0:T(8,128)(2,1)S(1)}, s16[272,1024]{1,0:T(8,128)(2,1)S(1)}, u32[]{:S(2)}, u32[]{:S(2)}) collective-permute-start(s16[272,1024]{1,0:T(8,128)(2,1)S(1)} %shard_map.61), channel_id=1, source_target_pairs={{0,2},{2,0},{4,6},{6,4},{8,10},{10,8},{12,14},{14,12},{16,18},{18,... | collective-permute-start | bytes 1671176 | tf_op jit(solution)/shard_map/ppermute | solution.py:225
  82.6 8.1 %collective-permute-done.9.refs_8_.refs_5_.refs_13_ = s16[272,1536]{1,0:T(8,128)(2,1)S(1)} collective-permute-done((s16[272,1536]{1,0:T(8,128)(2,1)S(1)}, s16[272,1536]{1,0:T(8,128)(2,1)S(1)}, u32[]{:S(2)}, u32[]{:S(2)}) %collective-permute-start.9) | collective-permute-done | bytes 835616 | tf_op jit(solution)/shard_map/ppermute | solution.py:225
  90.6 2.3 %shard_map.56 = s16[272,768]{1,0:T(8,128)(2,1)S(1)} custom-call(s32[256]{0:T(256)S(1)} %copy-done.1, s32[3]{0:T(128)S(1)} %pad_add_fusion.meta, bf16[272,512]{1,0:T(8,128)(2,1)S(1)} %pad.4.tok_own.tok_sib, bf16[272,512]{1,0:T(8,128)(2,1)S(1)} %pad.4.tok_own.tok_sib, bf16[256,32768]{1,0:T(8,128)(2,1)} %refs_17_.1, bf16[256,32768]{1,0:T(8,128)(2,1)} %refs_17_.1, ...), custom_call_target="tpu_custom_call" | custom-call | flops 213909504 | bytes 2039808 | tf_op jit(solution)/shard_map/pallas_call | solution.py:119
  93.0 2.3 %collective-permute-start.10 = (s16[272,768]{1,0:T(8,128)(2,1)S(1)}, s16[272,768]{1,0:T(8,128)(2,1)S(1)}, u32[]{:S(2)}, u32[]{:S(2)}) collective-permute-start(s16[272,768]{1,0:T(8,128)(2,1)S(1)} %shard_map.56), channel_id=1, source_target_pairs={{0,16},{2,18},{4,20},{6,22},{8,24},{10,26},{12,28},{14,30},{16,0},... | collective-permute-start | bytes 1253384 | tf_op jit(solution)/shard_map/ppermute | solution.py:225
  95.2 2.1 %shard_map.50 = s16[272,768]{1,0:T(8,128)(2,1)S(1)} custom-call(s32[256]{0:T(256)S(1)} %copy-done.1, s32[3]{0:T(128)S(1)} %pad_add_fusion.meta, bf16[272,512]{1,0:T(8,128)(2,1)S(1)} %pad.4.tok_own.tok_sib, bf16[272,512]{1,0:T(8,128)(2,1)S(1)} %pad.4.tok_own.tok_sib, bf16[256,32768]{1,0:T(8,128)(2,1)} %refs_17_.1, bf16[256,32768]{1,0:T(8,128)(2,1)} %refs_17_.1, ...), custom_call_target="tpu_custom_call" | custom-call | flops 213909504 | bytes 2039808 | tf_op jit(solution)/shard_map/pallas_call | solution.py:119
  98.5 1.9 %shard_map.62 = s16[272,512]{1,0:T(8,128)(2,1)S(1)} custom-call(s32[256]{0:T(256)S(1)} %copy-done.1, s32[3]{0:T(128)S(1)} %pad_add_fusion.meta, bf16[272,512]{1,0:T(8,128)(2,1)S(1)} %pad.4.tok_own.tok_sib, bf16[272,512]{1,0:T(8,128)(2,1)S(1)} %pad.4.tok_own.tok_sib, bf16[256,32768]{1,0:T(8,128)(2,1)} %refs_17_.1, bf16[256,32768]{1,0:T(8,128)(2,1)} %refs_17_.1, ...), custom_call_target="tpu_custom_call" | custom-call | flops 142606336 | bytes 1359872 | tf_op jit(solution)/shard_map/pallas_call | solution.py:119
  100.4 1.8 %collective-permute-start.16 = (s16[272,512]{1,0:T(8,128)(2,1)S(1)}, s16[272,512]{1,0:T(8,128)(2,1)S(1)}, u32[]{:S(2)}, u32[]{:S(2)}) collective-permute-start(s16[272,512]{1,0:T(8,128)(2,1)S(1)} %shard_map.62), channel_id=1, source_target_pairs={{0,4},{2,6},{4,0},{6,2},{8,12},{10,14},{12,8},{14,10},{16,20},{18,... | collective-permute-start | bytes 835592 | tf_op jit(solution)/shard_map/ppermute | solution.py:225
  102.3 9.6 %collective-permute-done.10.refs_6_.refs_14_ = s16[272,768]{1,0:T(8,128)(2,1)S(1)} collective-permute-done((s16[272,768]{1,0:T(8,128)(2,1)S(1)}, s16[272,768]{1,0:T(8,128)(2,1)S(1)}, u32[]{:S(2)}, u32[]{:S(2)}) %collective-permute-start.10) | collective-permute-done | bytes 417824 | tf_op jit(solution)/shard_map/ppermute | solution.py:225
  111.8 2.0 %shard_map.57 = s16[272,384]{1,0:T(8,128)(2,1)S(1)} custom-call(s32[256]{0:T(256)S(1)} %copy-done.1, s32[3]{0:T(128)S(1)} %pad_add_fusion.meta, bf16[272,512]{1,0:T(8,128)(2,1)S(1)} %pad.4.tok_own.tok_sib, bf16[272,512]{1,0:T(8,128)(2,1)S(1)} %pad.4.tok_own.tok_sib, bf16[256,32768]{1,0:T(8,128)(2,1)} %refs_17_.1, bf16[256,32768]{1,0:T(8,128)(2,1)} %refs_17_.1, ...), custom_call_target="tpu_custom_call" | custom-call | flops 106954752 | bytes 1228800 | tf_op jit(solution)/shard_map/pallas_call | solution.py:119
  113.8 1.5 %collective-permute-start.11 = (s16[272,384]{1,0:T(8,128)(2,1)S(1)}, s16[272,384]{1,0:T(8,128)(2,1)S(1)}, u32[]{:S(2)}, u32[]{:S(2)}) collective-permute-start(s16[272,384]{1,0:T(8,128)(2,1)S(1)} %shard_map.57), channel_id=1, source_target_pairs={{0,2},{2,0},{4,6},{6,4},{8,10},{10,8},{12,14},{14,12},{16,18},{18,... | collective-permute-start | bytes 626696 | tf_op jit(solution)/shard_map/ppermute | solution.py:225
  115.3 1.9 %shard_map.51 = s16[272,384]{1,0:T(8,128)(2,1)S(1)} custom-call(s32[256]{0:T(256)S(1)} %copy-done.1, s32[3]{0:T(128)S(1)} %pad_add_fusion.meta, bf16[272,512]{1,0:T(8,128)(2,1)S(1)} %pad.4.tok_own.tok_sib, bf16[272,512]{1,0:T(8,128)(2,1)S(1)} %pad.4.tok_own.tok_sib, bf16[256,32768]{1,0:T(8,128)(2,1)} %refs_17_.1, bf16[256,32768]{1,0:T(8,128)(2,1)} %refs_17_.1, ...), custom_call_target="tpu_custom_call" | custom-call | flops 106954752 | bytes 1228800 | tf_op jit(solution)/shard_map/pallas_call | solution.py:119
  118.1 1.7 %shard_map.63 = s16[272,256]{1,0:T(8,128)(2,1)S(1)} custom-call(s32[256]{0:T(256)S(1)} %copy-done.1, s32[3]{0:T(128)S(1)} %pad_add_fusion.meta, bf16[272,512]{1,0:T(8,128)(2,1)S(1)} %pad.4.tok_own.tok_sib, bf16[272,512]{1,0:T(8,128)(2,1)S(1)} %pad.4.tok_own.tok_sib, bf16[256,32768]{1,0:T(8,128)(2,1)} %refs_17_.1, bf16[256,32768]{1,0:T(8,128)(2,1)} %refs_17_.1, ...), custom_call_target="tpu_custom_call" | custom-call | flops 71303168 | bytes 819200 | tf_op jit(solution)/shard_map/pallas_call | solution.py:119
  119.8 2.2 %collective-permute-start.17 = (s16[272,256]{1,0:T(8,128)(2,1)S(1)}, s16[272,256]{1,0:T(8,128)(2,1)S(1)}, u32[]{:S(2)}, u32[]{:S(2)}) collective-permute-start(s16[272,256]{1,0:T(8,128)(2,1)S(1)} %shard_map.63), channel_id=1, source_target_pairs={{0,16},{2,18},{4,20},{6,22},{8,24},{10,26},{12,28},{14,30},{16,0},... | collective-permute-start | bytes 417800 | tf_op jit(solution)/shard_map/ppermute | solution.py:225
  122.0 11.9 %collective-permute-done.17.refs_22_ = s16[272,256]{1,0:T(8,128)(2,1)S(1)} collective-permute-done((s16[272,256]{1,0:T(8,128)(2,1)S(1)}, s16[272,256]{1,0:T(8,128)(2,1)S(1)}, u32[]{:S(2)}, u32[]{:S(2)}) %collective-permute-start.17) | collective-permute-done | bytes 139296 | tf_op jit(solution)/shard_map/ppermute | solution.py:225
  133.9 3.4 %shard_map.64 = bf16[256,1024]{1,0:T(8,128)(2,1)} custom-call(s32[256]{0:T(256)S(1)} %copy-done.1, s32[3]{0:T(128)S(1)} %pad_add_fusion.meta, bf16[272,512]{1,0:T(8,128)(2,1)S(1)} %pad.4.tok_own.tok_sib, bf16[272,512]{1,0:T(8,128)(2,1)S(1)} %pad.4.tok_own.tok_sib, bf16[256,32768]{1,0:T(8,128)(2,1)} %refs_17_.1, bf16[256,32768]{1,0:T(8,128)(2,1)} %refs_17_.1, ...), custom_call_target="tpu_custom_call" | custom-call | tf_op jit(solution)/shard_map/pallas_call | solution.py:180
  (36 shorter events, 8.8 us)
Async XLA Ops:
  0.7 0.7 copy-start
  4.8 3.3 %copy-start.2 = (bf16[16,8192]{1,0:T(8,128)(2,1)S(1)}, bf16[16,8192]{1,0:T(8,128)(2,1)}, u32[]{:S(2)}) copy-start(bf16[16,8192]{1,0:T(8,128)(2,1)} %param.5) | copy-start | bytes 786436
  4.8 12.4 %copy-start.1 = (s32[256]{0:T(256)S(1)}, s32[256]{0:T(256)}, u32[]{:S(2)}) copy-start(s32[256]{0:T(256)} %owner.37) | copy-start | bytes 3076
  4.8 22.6 %collective-permute-start.7 = (bf16[256,3072]{1,0:T(8,128)(2,1)}, bf16[256,3072]{1,0:T(8,128)(2,1)}, u32[]{:S(2)}, u32[]{:S(2)}) collective-permute-start(bf16[256,3072]{1,0:T(8,128)(2,1)} %shard_map.53), channel_id=1, source_target_pairs={{0,1},{1,0},{2,3},{3,2},{4,5},{5,4},{6,7},{7,6},{8,9},{9,8},{10,11... | collective-permute-start | bytes 4718600 | tf_op jit(solution)/shard_map/ppermute | solution.py:210
  8.0 25.3 %collective-permute-start.1 = (bf16[256,3072]{1,0:T(8,128)(2,1)S(1)}, bf16[256,3072]{1,0:T(8,128)(2,1)S(1)}, u32[]{:S(2)}, u32[]{:S(2)}) collective-permute-start(bf16[256,3072]{1,0:T(8,128)(2,1)S(1)} %shard_map.47), channel_id=1, source_target_pairs={{0,1},{1,0},{2,3},{3,2},{4,5},{5,4},{6,7},{7,6},{8,9},{9,8},{10,11... | collective-permute-start | bytes 4718600 | tf_op jit(solution)/shard_map/ppermute | solution.py:210
  8.9 18.4 %all-to-all-start = ((bf16[16,16,512]{2,0,1:T(8,128)(2,1)}), bf16[16,16,512]{2,0,1:T(8,128)(2,1)S(1)}, u32[]{:S(2)}, u32[]{:S(2)}) async-start(bf16[16,16,512]{2,0,1:T(8,128)(2,1)} %bitcast.12), calls=%async_computation | async-start | bytes 524288 | tf_op jit(solution)/shard_map/all_to_all | solution.py:213
  20.3 21.1 %collective-permute-start.13 = (bf16[256,2048]{1,0:T(8,128)(2,1)}, bf16[256,2048]{1,0:T(8,128)(2,1)}, u32[]{:S(2)}, u32[]{:S(2)}) collective-permute-start(bf16[256,2048]{1,0:T(8,128)(2,1)} %shard_map.59), channel_id=1, source_target_pairs={{0,1},{1,0},{2,3},{3,2},{4,5},{5,4},{6,7},{7,6},{8,9},{9,8},{10,11... | collective-permute-start | bytes 3145736 | tf_op jit(solution)/shard_map/ppermute | solution.py:210
  23.6 25.5 %collective-permute-start.6 = (bf16[256,3072]{1,0:T(8,128)(2,1)}, bf16[256,3072]{1,0:T(8,128)(2,1)}, u32[]{:S(2)}, u32[]{:S(2)}) collective-permute-start(bf16[256,3072]{1,0:T(8,128)(2,1)} %shard_map.52), channel_id=1, source_target_pairs={{0,1},{1,0},{2,3},{3,2},{4,5},{5,4},{6,7},{7,6},{8,9},{9,8},{10,11... | collective-permute-start | bytes 4718600 | tf_op jit(solution)/shard_map/ppermute | solution.py:211
  32.4 36.3 %collective-permute-start.8 = (s16[272,3072]{1,0:T(8,128)(2,1)S(1)}, s16[272,3072]{1,0:T(8,128)(2,1)S(1)}, u32[]{:S(2)}, u32[]{:S(2)}) collective-permute-start(s16[272,3072]{1,0:T(8,128)(2,1)S(1)} %shard_map.54), channel_id=1, source_target_pairs={{0,4},{2,6},{4,0},{6,2},{8,12},{10,14},{12,8},{14,10},{16,20},{18,... | collective-permute-start | bytes 5013512 | tf_op jit(solution)/shard_map/ppermute | solution.py:225
  38.0 36.1 %collective-permute-start.2 = (s16[272,3072]{1,0:T(8,128)(2,1)S(1)}, s16[272,3072]{1,0:T(8,128)(2,1)S(1)}, u32[]{:S(2)}, u32[]{:S(2)}) collective-permute-start(s16[272,3072]{1,0:T(8,128)(2,1)S(1)} %shard_map.48), channel_id=1, source_target_pairs={{0,2},{2,0},{4,6},{6,4},{8,10},{10,8},{12,14},{14,12},{16,18},{18,... | collective-permute-start | bytes 5013512 | tf_op jit(solution)/shard_map/ppermute | solution.py:225
  41.3 31.6 %collective-permute-start = (bf16[256,3072]{1,0:T(8,128)(2,1)S(1)}, bf16[256,3072]{1,0:T(8,128)(2,1)S(1)}, u32[]{:S(2)}, u32[]{:S(2)}) collective-permute-start(bf16[256,3072]{1,0:T(8,128)(2,1)S(1)} %shard_map.46), channel_id=1, source_target_pairs={{0,1},{1,0},{2,3},{3,2},{4,5},{5,4},{6,7},{7,6},{8,9},{9,8},{10,11... | collective-permute-start | bytes 4718600 | tf_op jit(solution)/shard_map/ppermute | solution.py:211
  45.7 32.4 %collective-permute-start.14 = (s16[272,2048]{1,0:T(8,128)(2,1)S(1)}, s16[272,2048]{1,0:T(8,128)(2,1)S(1)}, u32[]{:S(2)}, u32[]{:S(2)}) collective-permute-start(s16[272,2048]{1,0:T(8,128)(2,1)S(1)} %shard_map.60), channel_id=1, source_target_pairs={{0,8},{2,10},{4,12},{6,14},{8,0},{10,2},{12,4},{14,6},{16,24},{18,... | collective-permute-start | bytes 3342344 | tf_op jit(solution)/shard_map/ppermute | solution.py:225
  49.1 29.1 %collective-permute-start.12 = (bf16[256,2048]{1,0:T(8,128)(2,1)S(1)}, bf16[256,2048]{1,0:T(8,128)(2,1)S(1)}, u32[]{:S(2)}, u32[]{:S(2)}) collective-permute-start(bf16[256,2048]{1,0:T(8,128)(2,1)S(1)} %shard_map.58), channel_id=1, source_target_pairs={{0,1},{1,0},{2,3},{3,2},{4,5},{5,4},{6,7},{7,6},{8,9},{9,8},{10,11... | collective-permute-start | bytes 3145736 | tf_op jit(solution)/shard_map/ppermute | solution.py:211
  71.9 18.8 %collective-permute-start.9 = (s16[272,1536]{1,0:T(8,128)(2,1)S(1)}, s16[272,1536]{1,0:T(8,128)(2,1)S(1)}, u32[]{:S(2)}, u32[]{:S(2)}) collective-permute-start(s16[272,1536]{1,0:T(8,128)(2,1)S(1)} %shard_map.55), channel_id=1, source_target_pairs={{0,8},{2,10},{4,12},{6,14},{8,0},{10,2},{12,4},{14,6},{16,24},{18,... | collective-permute-start | bytes 2506760 | tf_op jit(solution)/shard_map/ppermute | solution.py:225
  77.0 18.2 %collective-permute-start.3 = (s16[272,1536]{1,0:T(8,128)(2,1)S(1)}, s16[272,1536]{1,0:T(8,128)(2,1)S(1)}, u32[]{:S(2)}, u32[]{:S(2)}) collective-permute-start(s16[272,1536]{1,0:T(8,128)(2,1)S(1)} %shard_map.49), channel_id=1, source_target_pairs={{0,4},{2,6},{4,0},{6,2},{8,12},{10,14},{12,8},{14,10},{16,20},{18,... | collective-permute-start | bytes 2506760 | tf_op jit(solution)/shard_map/ppermute | solution.py:225
  80.8 17.7 %collective-permute-start.15 = (s16[272,1024]{1,0:T(8,128)(2,1)S(1)}, s16[272,1024]{1,0:T(8,128)(2,1)S(1)}, u32[]{:S(2)}, u32[]{:S(2)}) collective-permute-start(s16[272,1024]{1,0:T(8,128)(2,1)S(1)} %shard_map.61), channel_id=1, source_target_pairs={{0,2},{2,0},{4,6},{6,4},{8,10},{10,8},{12,14},{14,12},{16,18},{18,... | collective-permute-start | bytes 1671176 | tf_op jit(solution)/shard_map/ppermute | solution.py:225
  93.0 18.8 %collective-permute-start.10 = (s16[272,768]{1,0:T(8,128)(2,1)S(1)}, s16[272,768]{1,0:T(8,128)(2,1)S(1)}, u32[]{:S(2)}, u32[]{:S(2)}) collective-permute-start(s16[272,768]{1,0:T(8,128)(2,1)S(1)} %shard_map.56), channel_id=1, source_target_pairs={{0,16},{2,18},{4,20},{6,22},{8,24},{10,26},{12,28},{14,30},{16,0},... | collective-permute-start | bytes 1253384 | tf_op jit(solution)/shard_map/ppermute | solution.py:225
  97.4 17.9 %collective-permute-start.4 = (s16[272,768]{1,0:T(8,128)(2,1)S(1)}, s16[272,768]{1,0:T(8,128)(2,1)S(1)}, u32[]{:S(2)}, u32[]{:S(2)}) collective-permute-start(s16[272,768]{1,0:T(8,128)(2,1)S(1)} %shard_map.50), channel_id=1, source_target_pairs={{0,8},{2,10},{4,12},{6,14},{8,0},{10,2},{12,4},{14,6},{16,24},{18,... | collective-permute-start | bytes 1253384 | tf_op jit(solution)/shard_map/ppermute | solution.py:225
  100.4 17.7 %collective-permute-start.16 = (s16[272,512]{1,0:T(8,128)(2,1)S(1)}, s16[272,512]{1,0:T(8,128)(2,1)S(1)}, u32[]{:S(2)}, u32[]{:S(2)}) collective-permute-start(s16[272,512]{1,0:T(8,128)(2,1)S(1)} %shard_map.62), channel_id=1, source_target_pairs={{0,4},{2,6},{4,0},{6,2},{8,12},{10,14},{12,8},{14,10},{16,20},{18,... | collective-permute-start | bytes 835592 | tf_op jit(solution)/shard_map/ppermute | solution.py:225
  113.8 20.1 %collective-permute-start.11 = (s16[272,384]{1,0:T(8,128)(2,1)S(1)}, s16[272,384]{1,0:T(8,128)(2,1)S(1)}, u32[]{:S(2)}, u32[]{:S(2)}) collective-permute-start(s16[272,384]{1,0:T(8,128)(2,1)S(1)} %shard_map.57), channel_id=1, source_target_pairs={{0,2},{2,0},{4,6},{6,4},{8,10},{10,8},{12,14},{14,12},{16,18},{18,... | collective-permute-start | bytes 626696 | tf_op jit(solution)/shard_map/ppermute | solution.py:225
  117.2 16.7 %collective-permute-start.5 = (s16[272,384]{1,0:T(8,128)(2,1)S(1)}, s16[272,384]{1,0:T(8,128)(2,1)S(1)}, u32[]{:S(2)}, u32[]{:S(2)}) collective-permute-start(s16[272,384]{1,0:T(8,128)(2,1)S(1)} %shard_map.51), channel_id=1, source_target_pairs={{0,16},{2,18},{4,20},{6,22},{8,24},{10,26},{12,28},{14,30},{16,0},... | collective-permute-start | bytes 626696 | tf_op jit(solution)/shard_map/ppermute | solution.py:225
  119.8 14.1 %collective-permute-start.17 = (s16[272,256]{1,0:T(8,128)(2,1)S(1)}, s16[272,256]{1,0:T(8,128)(2,1)S(1)}, u32[]{:S(2)}, u32[]{:S(2)}) collective-permute-start(s16[272,256]{1,0:T(8,128)(2,1)S(1)} %shard_map.63), channel_id=1, source_target_pairs={{0,16},{2,18},{4,20},{6,22},{8,24},{10,26},{12,28},{14,30},{16,0},... | collective-permute-start | bytes 417800 | tf_op jit(solution)/shard_map/ppermute | solution.py:225
